TPU v7x, 32 devices: a whole 2x2x4 slice. The times are simulated.
32 devices in a mesh: group: 2 (over x), pts: 16 (over z, y, core).
Axes of the slice: x: 2, y: 2, z: 4, core: 2. Of those that a mesh axis runs over, the one named last changes fastest.
Arguments:
- coords: int32 [3, 49152], P(None, ('group', 'pts')), parts along dimension 1, may hold values from 0 to 1023
- field: bfloat16 [64, 49152], P(None, ('group', 'pts')), parts along dimension 1, may hold values from -6 to 6
- mode_list: int32 [4096], replicated, may hold values from 0 to 4095, each once
- spec_weight: bfloat16 [2, 4096, 2, 64, 64], P(None, 'pts'), may hold values from -0.5 to 0.5
- bypass_weight: bfloat16 [2, 64, 64], replicated, may hold values from -0.75 to 0.75
- bypass_bias: float32 [2, 64], replicated, may hold values from -3 to 3
Outputs:
- output: bfloat16 [64, 49152], P(None, ('group', 'pts')), parts along dimension 1
There are 2 independent parts, one for each index of `group`. A program takes and returns all parts, laid end to end along the dimension named above; an argument that names none is the same for every part. Nothing has to cross between parts.
Inputs may be any that keep to these rules, and one draw needn't show every extreme that they name: `mode_list`: each of the 4096 mode numbers appears exactly once.
All inputs are finite; a program needn't handle non-finite values.
Results may differ from a plain program's by a relative error of at most 0.0059.
Values may be sent and summed in bfloat16 or wider, within the bound.
No kernel may reach another device: no remote copies, remote signals or barrier semaphores. Data moves between devices by JAX's collectives and lax.ppermute only.
A program may use at most 192 MiB of HBM per device.

v0:
```python
import math
import jax
import jax.numpy as jnp
from jax import lax
from jax.sharding import PartitionSpec as P

KDIM = 16
GRID = 1024
LAYERS = 2
TWO_PI = 2.0 * math.pi


def direct_basis(wave_ids, coords):
    centre = KDIM // 2
    wave_x = wave_ids // (KDIM * KDIM) - centre
    wave_y = wave_ids // KDIM % KDIM - centre
    wave_z = wave_ids % KDIM - centre
    phase_index = (
        wave_x[:, None] * coords[0][None, :]
        + wave_y[:, None] * coords[1][None, :]
        + wave_z[:, None] * coords[2][None, :]
    )
    phase_index = jnp.mod(phase_index, GRID)
    radians = phase_index.astype(jnp.float32) * (TWO_PI / GRID)
    return jnp.concatenate(
        [jnp.cos(radians).astype(jnp.bfloat16), (-jnp.sin(radians)).astype(jnp.bfloat16)], 0
    )


def mix_modes(spectrum, weights):
    width = weights.shape[-1]
    real_in = spectrum[:, :width]
    imag_in = spectrum[:, width:]
    weight_real = weights[:, 0].astype(jnp.float32)
    weight_imag = weights[:, 1].astype(jnp.float32)
    high = lax.Precision.HIGHEST
    real_out = jnp.einsum("kc,kcd->kd", real_in, weight_real, precision=high) - jnp.einsum(
        "kc,kcd->kd", imag_in, weight_imag, precision=high
    )
    imag_out = jnp.einsum("kc,kcd->kd", real_in, weight_imag, precision=high) + jnp.einsum(
        "kc,kcd->kd", imag_in, weight_real, precision=high
    )
    return jnp.concatenate([real_out, imag_out], 1).astype(jnp.bfloat16)


def finish_layer(spectral, field, layer_weight, layer_bias, modes_total):
    direct = lax.dot_general(
        layer_weight, field, (((0,), (0,)), ((), ())), preferred_element_type=jnp.float32
    )
    summed = spectral * (1.0 / math.sqrt(modes_total)) + direct + layer_bias[:, None]
    return jax.nn.gelu(summed, approximate=False).astype(jnp.bfloat16)


def body(coords, field, mode_list, spec_weight, bypass_weight, bypass_bias):
    width = field.shape[0]
    point_count = field.shape[1]
    modes_total = mode_list.shape[0]
    block_size = math.gcd(modes_total, 512)
    block_count = modes_total // block_size
    normaliser = 1.0 / math.sqrt(point_count * lax.axis_size("pts"))

    def basis_for(wave_ids):
        return direct_basis(wave_ids, coords)

    wave_blocks = mode_list.reshape(block_count, block_size)
    blocked = lax.map(basis_for, wave_blocks)
    basis = (
        blocked.reshape(block_count, 2, block_size, point_count)
        .transpose(1, 0, 2, 3)
        .reshape(2 * modes_total, point_count)
    )
    for depth in range(LAYERS):
        current = field
        product = (
            lax.dot_general(
                basis, current, (((1,), (1,)), ((), ())), preferred_element_type=jnp.float32
            )
            * normaliser
        )
        partial_spectrum = jnp.concatenate([product[:modes_total], product[modes_total:]], 1)
        spectrum = lax.psum_scatter(partial_spectrum, "pts", scatter_dimension=0, tiled=True)
        mixed = mix_modes(spectrum, spec_weight[depth])
        gathered = lax.all_gather(mixed, "pts", axis=0, tiled=True)
        stacked = jnp.concatenate([gathered[:, :width], gathered[:, width:]], 0)
        spectral = lax.dot_general(
            stacked, basis, (((0,), (0,)), ((), ())), preferred_element_type=jnp.float32
        )
        field = finish_layer(
            spectral, current, bypass_weight[depth], bypass_bias[depth], modes_total
        )
    return field


def solution(mesh):
    placed = (
        P(None, ("group", "pts")),
        P(None, ("group", "pts")),
        P(),
        P(None, "pts", None, None, None),
        P(),
        P(),
    )
    return jax.shard_map(
        body, mesh=mesh, in_specs=placed, out_specs=P(None, ("group", "pts")), check_vma=False
    )
```

profile of v0, /device:TPU:0, one launch (start us, length us, event | category | flops | bytes accessed | tf_op | source)
XLA Modules:
  0.0 433.3 jit_solution(10487194853132339083)
XLA Ops:
  6.5 0.8 reshape.100
  7.3 131.8 %while.13 = (s32[]{:T(128)}, bf16[8,1024,1536]{2,1,0:T(8,128)(2,1)}, s32[8,512]{1,0:T(8,128)S(1)}, s32[3,1536]{1,0:T(4,128)}, s32[]{:T(128)}) while((s32[]{:T(128)}, bf16[8,1024,1536]{2,1,0:T(8,128)(2,1)}, s32[8,512]{1,0:T(8,128)S(1)}, s32[3,1536]{1,0:T(4,128)}, s32[]{:T(128)}) %tuple.57), condition=%wide.region_1.2_spmd, body=%wide.region_0.1_spmd.sunk | while | flops 22828544 | bytes 9511489 | solution.py:66
  7.3 0.9 slice_reduce_fusion.4
  8.2 13.6 %cosine_convert_fusion.2 = (bf16[512,1536]{1,0:T(8,128)(2,1)S(1)}, bf16[512,1536]{1,0:T(8,128)(2,1)S(1)}) fusion(s32[1536]{0:T(1024)S(1)} %get-tuple-element.177, s32[512]{0:T(512)S(1)} %get-tuple-element.178, s32[1536]{0:T(1024)S(1)} %get-tuple-element.179, s32[512]{0:T(512)S(1)} %get-tuple-element.180, s32[1536]{0:T(1024)S(1)} %get-tuple-element.181, ...), kind=kLoop, calls=%fused_computation.9.clone.1 | loop fusion | flops 16515072 | bytes 3170304 | tf_op jit(solution)/shard_map/while/body/eval_jaxpr/convert_element_type | solution.py:26
  21.9 2.0 fusion.71
  23.9 0.9 slice_reduce_fusion.4
  24.8 13.6 %cosine_convert_fusion.2 = (bf16[512,1536]{1,0:T(8,128)(2,1)S(1)}, bf16[512,1536]{1,0:T(8,128)(2,1)S(1)}) fusion(s32[1536]{0:T(1024)S(1)} %get-tuple-element.177, s32[512]{0:T(512)S(1)} %get-tuple-element.178, s32[1536]{0:T(1024)S(1)} %get-tuple-element.179, s32[512]{0:T(512)S(1)} %get-tuple-element.180, s32[1536]{0:T(1024)S(1)} %get-tuple-element.181, ...), kind=kLoop, calls=%fused_computation.9.clone.1 | loop fusion | flops 16515072 | bytes 3170304 | tf_op jit(solution)/shard_map/while/body/eval_jaxpr/convert_element_type | solution.py:26
  38.4 2.0 fusion.71
  40.4 0.9 slice_reduce_fusion.4
  41.3 13.6 %cosine_convert_fusion.2 = (bf16[512,1536]{1,0:T(8,128)(2,1)S(1)}, bf16[512,1536]{1,0:T(8,128)(2,1)S(1)}) fusion(s32[1536]{0:T(1024)S(1)} %get-tuple-element.177, s32[512]{0:T(512)S(1)} %get-tuple-element.178, s32[1536]{0:T(1024)S(1)} %get-tuple-element.179, s32[512]{0:T(512)S(1)} %get-tuple-element.180, s32[1536]{0:T(1024)S(1)} %get-tuple-element.181, ...), kind=kLoop, calls=%fused_computation.9.clone.1 | loop fusion | flops 16515072 | bytes 3170304 | tf_op jit(solution)/shard_map/while/body/eval_jaxpr/convert_element_type | solution.py:26
  54.9 1.8 fusion.71
  56.8 0.9 slice_reduce_fusion.4
  57.7 13.6 %cosine_convert_fusion.2 = (bf16[512,1536]{1,0:T(8,128)(2,1)S(1)}, bf16[512,1536]{1,0:T(8,128)(2,1)S(1)}) fusion(s32[1536]{0:T(1024)S(1)} %get-tuple-element.177, s32[512]{0:T(512)S(1)} %get-tuple-element.178, s32[1536]{0:T(1024)S(1)} %get-tuple-element.179, s32[512]{0:T(512)S(1)} %get-tuple-element.180, s32[1536]{0:T(1024)S(1)} %get-tuple-element.181, ...), kind=kLoop, calls=%fused_computation.9.clone.1 | loop fusion | flops 16515072 | bytes 3170304 | tf_op jit(solution)/shard_map/while/body/eval_jaxpr/convert_element_type | solution.py:26
  71.4 1.9 fusion.71
  73.3 0.9 slice_reduce_fusion.4
  74.2 13.6 %cosine_convert_fusion.2 = (bf16[512,1536]{1,0:T(8,128)(2,1)S(1)}, bf16[512,1536]{1,0:T(8,128)(2,1)S(1)}) fusion(s32[1536]{0:T(1024)S(1)} %get-tuple-element.177, s32[512]{0:T(512)S(1)} %get-tuple-element.178, s32[1536]{0:T(1024)S(1)} %get-tuple-element.179, s32[512]{0:T(512)S(1)} %get-tuple-element.180, s32[1536]{0:T(1024)S(1)} %get-tuple-element.181, ...), kind=kLoop, calls=%fused_computation.9.clone.1 | loop fusion | flops 16515072 | bytes 3170304 | tf_op jit(solution)/shard_map/while/body/eval_jaxpr/convert_element_type | solution.py:26
  87.9 1.8 fusion.71
  89.7 0.9 slice_reduce_fusion.4
  90.6 13.6 %cosine_convert_fusion.2 = (bf16[512,1536]{1,0:T(8,128)(2,1)S(1)}, bf16[512,1536]{1,0:T(8,128)(2,1)S(1)}) fusion(s32[1536]{0:T(1024)S(1)} %get-tuple-element.177, s32[512]{0:T(512)S(1)} %get-tuple-element.178, s32[1536]{0:T(1024)S(1)} %get-tuple-element.179, s32[512]{0:T(512)S(1)} %get-tuple-element.180, s32[1536]{0:T(1024)S(1)} %get-tuple-element.181, ...), kind=kLoop, calls=%fused_computation.9.clone.1 | loop fusion | flops 16515072 | bytes 3170304 | tf_op jit(solution)/shard_map/while/body/eval_jaxpr/convert_element_type | solution.py:26
  104.3 1.9 fusion.71
  106.2 0.9 slice_reduce_fusion.4
  107.1 13.6 %cosine_convert_fusion.2 = (bf16[512,1536]{1,0:T(8,128)(2,1)S(1)}, bf16[512,1536]{1,0:T(8,128)(2,1)S(1)}) fusion(s32[1536]{0:T(1024)S(1)} %get-tuple-element.177, s32[512]{0:T(512)S(1)} %get-tuple-element.178, s32[1536]{0:T(1024)S(1)} %get-tuple-element.179, s32[512]{0:T(512)S(1)} %get-tuple-element.180, s32[1536]{0:T(1024)S(1)} %get-tuple-element.181, ...), kind=kLoop, calls=%fused_computation.9.clone.1 | loop fusion | flops 16515072 | bytes 3170304 | tf_op jit(solution)/shard_map/while/body/eval_jaxpr/convert_element_type | solution.py:26
  120.7 1.9 fusion.71
  122.7 0.9 slice_reduce_fusion.4
  123.6 13.6 %cosine_convert_fusion.2 = (bf16[512,1536]{1,0:T(8,128)(2,1)S(1)}, bf16[512,1536]{1,0:T(8,128)(2,1)S(1)}) fusion(s32[1536]{0:T(1024)S(1)} %get-tuple-element.177, s32[512]{0:T(512)S(1)} %get-tuple-element.178, s32[1536]{0:T(1024)S(1)} %get-tuple-element.179, s32[512]{0:T(512)S(1)} %get-tuple-element.180, s32[1536]{0:T(1024)S(1)} %get-tuple-element.181, ...), kind=kLoop, calls=%fused_computation.9.clone.1 | loop fusion | flops 16515072 | bytes 3170304 | tf_op jit(solution)/shard_map/while/body/eval_jaxpr/convert_element_type | solution.py:26
  137.2 1.8 fusion.71
  139.1 20.8 %copy.7 = bf16[2,8,512,1536]{3,2,1,0:T(8,128)(2,1)} copy(bf16[2,8,512,1536]{3,2,0,1:T(8,128)(2,1)} %bitcast.65) | data formatting | bytes 50331648 | tf_op jit(solution)/shard_map/transpose | solution.py:69
  159.9 12.3 %convolution_multiply_fusion.1 = f32[8192,64]{0,1:T(8,128)S(1)} fusion(bf16[8192,1536]{1,0:T(8,128)(2,1)} %bitcast.61, bf16[64,1536]{1,0:T(8,128)(2,1)S(1)} %copy-done), kind=kOutput, calls=%fused_computation.33 | convolution fusion | flops 1611137024 | bytes 27459584 | tf_op jit(solution)/shard_map/dot_general | solution.py:75
  172.4 1.5 pad_maximum_fusion
  174.0 6.0 %slice_bitcast_fusion = (bf16[256,2,64,64]{0,3,2,1:T(8,128)(2,1)}, bf16[256,2,64,64]{0,3,2,1:T(8,128)(2,1)}) fusion(bf16[2,256,2,64,64]{1,4,3,2,0:T(8,128)(2,1)} %param.11), kind=kLoop, calls=%fused_computation.50 | loop fusion | bytes 16777216 | tf_op jit(solution)/shard_map/squeeze | solution.py:82
  180.0 58.3 %reduce-scatter.3.cloned.1.call-done = f32[256,128]{0,1:T(8,128)} async-done(((f32[4096,128]{0,1:T(8,128)}), f32[256,128]{0,1:T(8,128)}) %reduce-scatter.3.cloned.1.call-update) | async-done | bytes 131088 | tf_op jit(solution)/shard_map/reduce_scatter | solution.py:81
  238.3 0.9 fusion.59
  239.2 3.0 fusion.11
  242.7 0.7 pad_maximum_fusion.2
  243.7 36.9 %all-gather.3.cloned.1.call-done = bf16[4096,128]{1,0:T(8,128)(2,1)} async-done(((bf16[256,128]{1,0:T(8,128)(2,1)}), bf16[4096,128]{1,0:T(8,128)(2,1)}) %all-gather.3.cloned.1.call-update) | async-done | bytes 1048592 | tf_op jit(solution)/shard_map/all_gather | solution.py:83
  280.5 2.1 fusion.57
  282.6 10.1 %convolution_multiply_fusion.3 = f32[64,1536]{1,0:T(8,128)S(1)} fusion(bf16[8192,1536]{1,0:T(8,128)(2,1)} %bitcast.62, bf16[4096,64]{1,0:T(8,128)(2,1)S(1)} %get-tuple-element.135, bf16[4096,64]{1,0:T(8,128)(2,1)S(1)} %get-tuple-element.134), kind=kOutput, calls=%fused_computation.57 | convolution fusion | flops 1612808192 | bytes 26607616 | tf_op jit(solution)/shard_map/dot_general | solution.py:85
  292.7 1.0 fusion.28
  293.8 12.3 %convolution_multiply_fusion = f32[8192,64]{0,1:T(8,128)S(1)} fusion(bf16[8192,1536]{1,0:T(8,128)(2,1)} %bitcast.63, bf16[64,1536]{1,0:T(8,128)(2,1)S(1)} %fusion.28), kind=kOutput, calls=%fused_computation.32 | convolution fusion | flops 1611137024 | bytes 27459584 | tf_op jit(solution)/shard_map/dot_general | solution.py:75
  306.3 1.5 pad_maximum_fusion.1
  307.8 60.6 %reduce-scatter.5.cloned.1.call-done = f32[256,128]{0,1:T(8,128)} async-done(((f32[4096,128]{0,1:T(8,128)}), f32[256,128]{0,1:T(8,128)}) %reduce-scatter.5.cloned.1.call-update) | async-done | bytes 131088 | tf_op jit(solution)/shard_map/reduce_scatter | solution.py:81
  368.5 0.9 fusion.58
  369.3 3.0 fusion.15
  372.8 0.7 pad_maximum_fusion.3
  373.5 0.2 convolution_bitcast_fusion
  373.8 36.8 %all-gather.5.cloned.1.call-done = bf16[4096,128]{1,0:T(8,128)(2,1)} async-done(((bf16[256,128]{1,0:T(8,128)(2,1)}), bf16[4096,128]{1,0:T(8,128)(2,1)}) %all-gather.5.cloned.1.call-update) | async-done | bytes 1048592 | tf_op jit(solution)/shard_map/all_gather | solution.py:83
  410.6 2.1 fusion.56
  412.7 14.1 %fusion.31 = bf16[64,1536]{1,0:T(8,128)(2,1)} fusion(f32[64,1536]{1,0:T(8,128)S(1)} %convolution_bitcast_fusion, bf16[8192,1536]{1,0:T(8,128)(2,1)} %bitcast.64, bf16[4096,64]{1,0:T(8,128)(2,1)S(1)} %get-tuple-element.133, bf16[4096,64]{1,0:T(8,128)(2,1)S(1)} %get-tuple-element.132, f32[64]{0:T(128)S(1)} %get-tuple-element.140), kind=kOutput, calls=%fused_computation.78 | convolution fusion | flops 1619394560 | bytes 26804480 | tf_op jit(solution)/shard_map/dot_general | solution.py:85
  (45 shorter events, 1.7 us)
Async XLA Ops:
  6.5 153.4 %copy-start = (bf16[64,1536]{1,0:T(8,128)(2,1)S(1)}, bf16[64,1536]{1,0:T(8,128)(2,1)}, u32[]{:S(2)}) copy-start(bf16[64,1536]{1,0:T(8,128)(2,1)} %param.9) | copy-start | bytes 589828
  6.5 231.8 %reduce-scatter.3.cloned.1.call-start = ((), (), s32[]{:S(2)}) async-start(), calls=%async_computation.2 | async-start | bytes 2228224 | tf_op jit(solution)/shard_map/reduce_scatter | solution.py:81
  173.9 106.6 %all-gather.3.cloned.1.call-start = ((), (), s32[]{:S(2)}) async-start(), calls=%async_computation.3 | async-start | bytes 1114112 | tf_op jit(solution)/shard_map/all_gather | solution.py:83
  239.2 4.4 %copy-start.2 = (f32[2,64]{1,0:T(2,128)S(1)}, f32[2,64]{1,0:T(2,128)}, u32[]{:S(2)}) copy-start(f32[2,64]{1,0:T(2,128)} %param.13) | copy-start | bytes 1540
  243.4 125.1 %reduce-scatter.5.cloned.1.call-start = ((), (), s32[]{:S(2)}) async-start(), calls=%async_computation.4 | async-start | bytes 2228224 | tf_op jit(solution)/shard_map/reduce_scatter | solution.py:81
  282.6 10.1 %copy-start.1 = (bf16[2,64,64]{2,1,0:T(8,128)(2,1)S(1)}, bf16[2,64,64]{2,1,0:T(8,128)(2,1)}, u32[]{:S(2)}) copy-start(bf16[2,64,64]{2,1,0:T(8,128)(2,1)} %param.12) | copy-start | bytes 49156
  307.8 102.8 %all-gather.5.cloned.1.call-start = ((), (), s32[]{:S(2)}) async-start(), calls=%async_computation.5 | async-start | bytes 1114112 | tf_op jit(solution)/shard_map/all_gather | solution.py:83
Sparse Core Ops, SparseCore 0:
  174.0 64.2 reduce-scatter.2
  243.5 36.9 all-gather.2
  307.9 60.5 reduce-scatter.4
  373.7 36.8 all-gather.4
where the time goes:
time: 434 us; the launch traced here: 433 us
  waiting for transfers between devices  193 us (44%)
  other arithmetic  135 us (31%)
  matrix products  50.2 us (12%)
  local copies, waits for them, and re-layouts  41.8 us (10%)
  between operations  13.3 us (3%)
    reduce_scatter x2, waiting for transfers between devices, body(): lax.psum_scatter(partial_spectrum, 'pts', scatter_dimension=0, tiled=True)  119 us
    convert_element_type x8, other arithmetic, direct_basis(): jnp.cos(radians).astype(jnp.bfloat16)  109 us
    all_gather x2, waiting for transfers between devices, body(): gathered = lax.all_gather(mixed, 'pts', axis=0, tiled=True)  73.7 us
    dot_general x2, matrix products, body(): lax.dot_general(basis, current, (((1,), (1,)), ((), ())), preferred_eleme...  24.7 us
    dot_general x2, matrix products, body(): lax.dot_general(stacked, basis, (((0,), (0,)), ((), ())), preferred_eleme...  24.2 us
    transpose x1, local copies, waits for them, and re-layouts, body(): basis = blocked.reshape(block_count, 2, block_size, point_count).transpos...  20.8 us
    dynamic_update_slice x8, other arithmetic, body(): blocked = lax.map(basis_for, wave_blocks)  15.2 us
  transfers between devices with their start and end apart: 4, of which 4 were waited for; matrix products, arithmetic and copies ran while one was open for 1% of the time, Pallas kernels for 0%

commit v1 on v0

--- a/solution.py
+++ b/solution.py
@@ -80,7 +80,16 @@
         partial_spectrum = jnp.concatenate([product[:modes_total], product[modes_total:]], 1)
         spectrum = lax.psum_scatter(partial_spectrum, "pts", scatter_dimension=0, tiled=True)
         mixed = mix_modes(spectrum, spec_weight[depth])
-        gathered = lax.all_gather(mixed, "pts", axis=0, tiled=True)
+        ways = lax.axis_size("pts")
+        up = [(d, (d + 1) % ways) for d in range(ways)]
+        down = [(d, (d - 1) % ways) for d in range(ways)]
+        earlier, later = ([mixed], [mixed])
+        for _ in range(ways // 2):
+            earlier.append(lax.ppermute(earlier[-1], "pts", up))
+        for _ in range((ways - 1) // 2):
+            later.append(lax.ppermute(later[-1], "pts", down))
+        line = jnp.concatenate([*earlier[::-1], *later[1:]], axis=0)
+        gathered = jnp.roll(line, (lax.axis_index("pts") - ways // 2) * mixed.shape[0], axis=0)
         stacked = jnp.concatenate([gathered[:, :width], gathered[:, width:]], 0)
         spectral = lax.dot_general(
             stacked, basis, (((0,), (0,)), ((), ())), preferred_element_type=jnp.float32

time: 434 us -> 468 us (1.078)
  starting transfers between devices: 0.31 us -> 63.2 us
  waiting for transfers between devices: 193 us -> 160 us
  other arithmetic: 135 us -> 141 us
    all_gather x2 -> x0, waiting for transfers between devices: 73.7 us -> none  [body(): gathered = lax.all_gather(mixed, 'pts', axis=0, tiled=True)]
    ppermute x0 -> x30, starting transfers between devices: none -> 63.2 us  [the longest x14 63 us: body(): later.append(lax.ppermute(later[-1], 'pts', down))]
    ppermute x0 -> x30, waiting for transfers between devices: none -> 39.2 us  [the longest x16 38.9 us: body(): earlier.append(lax.ppermute(earlier[-1], 'pts', up))]
    concatenate x0 -> x2, other arithmetic: none -> 7.31 us  [body(): jnp.roll(line, (lax.axis_index('pts') - ways // 2) * mixed.shape[0], axis=0)]
  transfers between devices with their start and end apart: 4 -> 32, of which waited for: 4 -> 19; matrix products, arithmetic and copies ran while one was open for 1% -> 1% of each run, Pallas kernels for 0% -> 0%
where the time goes in v1:
time: 468 us
  waiting for transfers between devices  160 us (34%)
  other arithmetic  141 us (30%)
  starting transfers between devices  63.2 us (14%)
  matrix products  50.2 us (11%)
  local copies, waits for them, and re-layouts  38.8 us (8%)
  between operations  13.8 us (3%)
    reduce_scatter x2, waiting for transfers between devices, body(): lax.psum_scatter(partial_spectrum, 'pts', scatter_dimension=0, tiled=True)  121 us
    convert_element_type x8, other arithmetic, direct_basis(): jnp.cos(radians).astype(jnp.bfloat16)  109 us
    ppermute x14, starting transfers between devices, body(): later.append(lax.ppermute(later[-1], 'pts', down))  63 us
    ppermute x16, waiting for transfers between devices, body(): earlier.append(lax.ppermute(earlier[-1], 'pts', up))  38.9 us
    dot_general x2, matrix products, body(): lax.dot_general(basis, current, (((1,), (1,)), ((), ())), preferred_eleme...  24.7 us
    dot_general x2, matrix products, body(): lax.dot_general(stacked, basis, (((0,), (0,)), ((), ())), preferred_eleme...  24.2 us
    transpose x1, local copies, waits for them, and re-layouts, body(): basis = blocked.reshape(block_count, 2, block_size, point_count).transpos...  20.8 us
    dynamic_update_slice x8, other arithmetic, body(): blocked = lax.map(basis_for, wave_blocks)  15.2 us
  transfers between devices with their start and end apart: 32, of which 19 were waited for; matrix products, arithmetic and copies ran while one was open for 1% of the time, Pallas kernels for 0%

profile of v1, /device:TPU:0, one launch (start us, length us, event | category | flops | bytes accessed | tf_op | source)
XLA Modules:
  0.0 467.5 jit_solution(4201541463412921354)
XLA Ops:
  7.3 131.7 %while.13 = (s32[]{:T(128)}, bf16[8,1024,1536]{2,1,0:T(8,128)(2,1)}, s32[8,512]{1,0:T(8,128)S(1)}, s32[3,1536]{1,0:T(4,128)}, s32[]{:T(128)}) while((s32[]{:T(128)}, bf16[8,1024,1536]{2,1,0:T(8,128)(2,1)}, s32[8,512]{1,0:T(8,128)S(1)}, s32[3,1536]{1,0:T(4,128)}, s32[]{:T(128)}) %tuple.58), condition=%wide.region_1.2_spmd, body=%wide.region_0.1_spmd.sunk | while | flops 22828544 | bytes 9511489 | solution.py:66
  8.2 13.6 %cosine_convert_fusion.2 = (bf16[512,1536]{1,0:T(8,128)(2,1)S(1)}, bf16[512,1536]{1,0:T(8,128)(2,1)S(1)}) fusion(s32[1536]{0:T(1024)S(1)} %get-tuple-element.178, s32[512]{0:T(512)S(1)} %get-tuple-element.179, s32[1536]{0:T(1024)S(1)} %get-tuple-element.180, s32[512]{0:T(512)S(1)} %get-tuple-element.181, s32[1536]{0:T(1024)S(1)} %get-tuple-element.182, ...), kind=kLoop, calls=%fused_computation.9.clone.1 | loop fusion | flops 16515072 | bytes 3170304 | tf_op jit(solution)/shard_map/while/body/eval_jaxpr/convert_element_type | solution.py:26
  21.9 1.9 fusion.73
  24.7 13.6 %cosine_convert_fusion.2 = (bf16[512,1536]{1,0:T(8,128)(2,1)S(1)}, bf16[512,1536]{1,0:T(8,128)(2,1)S(1)}) fusion(s32[1536]{0:T(1024)S(1)} %get-tuple-element.178, s32[512]{0:T(512)S(1)} %get-tuple-element.179, s32[1536]{0:T(1024)S(1)} %get-tuple-element.180, s32[512]{0:T(512)S(1)} %get-tuple-element.181, s32[1536]{0:T(1024)S(1)} %get-tuple-element.182, ...), kind=kLoop, calls=%fused_computation.9.clone.1 | loop fusion | flops 16515072 | bytes 3170304 | tf_op jit(solution)/shard_map/while/body/eval_jaxpr/convert_element_type | solution.py:26
  38.4 1.9 fusion.73
  41.2 13.6 %cosine_convert_fusion.2 = (bf16[512,1536]{1,0:T(8,128)(2,1)S(1)}, bf16[512,1536]{1,0:T(8,128)(2,1)S(1)}) fusion(s32[1536]{0:T(1024)S(1)} %get-tuple-element.178, s32[512]{0:T(512)S(1)} %get-tuple-element.179, s32[1536]{0:T(1024)S(1)} %get-tuple-element.180, s32[512]{0:T(512)S(1)} %get-tuple-element.181, s32[1536]{0:T(1024)S(1)} %get-tuple-element.182, ...), kind=kLoop, calls=%fused_computation.9.clone.1 | loop fusion | flops 16515072 | bytes 3170304 | tf_op jit(solution)/shard_map/while/body/eval_jaxpr/convert_element_type | solution.py:26
  57.6 13.6 %cosine_convert_fusion.2 = (bf16[512,1536]{1,0:T(8,128)(2,1)S(1)}, bf16[512,1536]{1,0:T(8,128)(2,1)S(1)}) fusion(s32[1536]{0:T(1024)S(1)} %get-tuple-element.178, s32[512]{0:T(512)S(1)} %get-tuple-element.179, s32[1536]{0:T(1024)S(1)} %get-tuple-element.180, s32[512]{0:T(512)S(1)} %get-tuple-element.181, s32[1536]{0:T(1024)S(1)} %get-tuple-element.182, ...), kind=kLoop, calls=%fused_computation.9.clone.1 | loop fusion | flops 16515072 | bytes 3170304 | tf_op jit(solution)/shard_map/while/body/eval_jaxpr/convert_element_type | solution.py:26
  71.3 2.0 fusion.73
  74.2 13.6 %cosine_convert_fusion.2 = (bf16[512,1536]{1,0:T(8,128)(2,1)S(1)}, bf16[512,1536]{1,0:T(8,128)(2,1)S(1)}) fusion(s32[1536]{0:T(1024)S(1)} %get-tuple-element.178, s32[512]{0:T(512)S(1)} %get-tuple-element.179, s32[1536]{0:T(1024)S(1)} %get-tuple-element.180, s32[512]{0:T(512)S(1)} %get-tuple-element.181, s32[1536]{0:T(1024)S(1)} %get-tuple-element.182, ...), kind=kLoop, calls=%fused_computation.9.clone.1 | loop fusion | flops 16515072 | bytes 3170304 | tf_op jit(solution)/shard_map/while/body/eval_jaxpr/convert_element_type | solution.py:26
  90.6 13.6 %cosine_convert_fusion.2 = (bf16[512,1536]{1,0:T(8,128)(2,1)S(1)}, bf16[512,1536]{1,0:T(8,128)(2,1)S(1)}) fusion(s32[1536]{0:T(1024)S(1)} %get-tuple-element.178, s32[512]{0:T(512)S(1)} %get-tuple-element.179, s32[1536]{0:T(1024)S(1)} %get-tuple-element.180, s32[512]{0:T(512)S(1)} %get-tuple-element.181, s32[1536]{0:T(1024)S(1)} %get-tuple-element.182, ...), kind=kLoop, calls=%fused_computation.9.clone.1 | loop fusion | flops 16515072 | bytes 3170304 | tf_op jit(solution)/shard_map/while/body/eval_jaxpr/convert_element_type | solution.py:26
  104.2 1.9 fusion.73
  107.0 13.6 %cosine_convert_fusion.2 = (bf16[512,1536]{1,0:T(8,128)(2,1)S(1)}, bf16[512,1536]{1,0:T(8,128)(2,1)S(1)}) fusion(s32[1536]{0:T(1024)S(1)} %get-tuple-element.178, s32[512]{0:T(512)S(1)} %get-tuple-element.179, s32[1536]{0:T(1024)S(1)} %get-tuple-element.180, s32[512]{0:T(512)S(1)} %get-tuple-element.181, s32[1536]{0:T(1024)S(1)} %get-tuple-element.182, ...), kind=kLoop, calls=%fused_computation.9.clone.1 | loop fusion | flops 16515072 | bytes 3170304 | tf_op jit(solution)/shard_map/while/body/eval_jaxpr/convert_element_type | solution.py:26
  120.7 2.0 fusion.73
  123.6 13.6 %cosine_convert_fusion.2 = (bf16[512,1536]{1,0:T(8,128)(2,1)S(1)}, bf16[512,1536]{1,0:T(8,128)(2,1)S(1)}) fusion(s32[1536]{0:T(1024)S(1)} %get-tuple-element.178, s32[512]{0:T(512)S(1)} %get-tuple-element.179, s32[1536]{0:T(1024)S(1)} %get-tuple-element.180, s32[512]{0:T(512)S(1)} %get-tuple-element.181, s32[1536]{0:T(1024)S(1)} %get-tuple-element.182, ...), kind=kLoop, calls=%fused_computation.9.clone.1 | loop fusion | flops 16515072 | bytes 3170304 | tf_op jit(solution)/shard_map/while/body/eval_jaxpr/convert_element_type | solution.py:26
  139.0 20.8 %copy.7 = bf16[2,8,512,1536]{3,2,1,0:T(8,128)(2,1)} copy(bf16[2,8,512,1536]{3,2,0,1:T(8,128)(2,1)} %bitcast.65) | data formatting | bytes 50331648 | tf_op jit(solution)/shard_map/transpose | solution.py:69
  159.8 12.3 %convolution_multiply_fusion.1 = f32[8192,64]{0,1:T(8,128)S(1)} fusion(bf16[8192,1536]{1,0:T(8,128)(2,1)} %bitcast.61, bf16[64,1536]{1,0:T(8,128)(2,1)S(1)} %copy-done), kind=kOutput, calls=%fused_computation.33 | convolution fusion | flops 1611137024 | bytes 27459584 | tf_op jit(solution)/shard_map/dot_general | solution.py:75
  173.9 6.0 %slice_bitcast_fusion = (bf16[256,2,64,64]{0,3,2,1:T(8,128)(2,1)}, bf16[256,2,64,64]{0,3,2,1:T(8,128)(2,1)}) fusion(bf16[2,256,2,64,64]{1,4,3,2,0:T(8,128)(2,1)} %param.13), kind=kLoop, calls=%fused_computation.50 | loop fusion | bytes 16777216 | tf_op jit(solution)/shard_map/squeeze | solution.py:82
  179.9 58.3 %reduce-scatter.3.cloned.1.call-done = f32[256,128]{0,1:T(8,128)} async-done(((f32[4096,128]{0,1:T(8,128)}), f32[256,128]{0,1:T(8,128)}) %reduce-scatter.3.cloned.1.call-update) | async-done | bytes 131088 | tf_op jit(solution)/shard_map/reduce_scatter | solution.py:81
  239.1 3.0 fusion.11
  242.7 6.4 %collective-permute-done = bf16[256,128]{1,0:T(8,128)(2,1)S(1)} collective-permute-done((bf16[256,128]{1,0:T(8,128)(2,1)S(1)}, bf16[256,128]{1,0:T(8,128)(2,1)S(1)}, u32[]{:S(2)}, u32[]{:S(2)}) %collective-permute-start) | collective-permute-done | bytes 65568 | tf_op jit(solution)/shard_map/ppermute | solution.py:88
  249.1 4.4 collective-permute-start.8
  253.5 2.0 collective-permute-done.1
  255.6 4.4 collective-permute-start.9
  260.0 1.9 collective-permute-done.2
  261.9 4.5 collective-permute-start.10
  268.4 4.5 collective-permute-start.11
  274.7 4.5 collective-permute-start.12
  279.2 1.9 collective-permute-done.5
  281.1 4.5 collective-permute-start.13
  285.6 1.9 collective-permute-done.6
  287.5 4.6 collective-permute-start.14
  294.3 3.7 fusion.27
  298.3 10.1 %convolution_multiply_fusion.3 = f32[64,1536]{1,0:T(8,128)S(1)} fusion(bf16[8192,1536]{1,0:T(8,128)(2,1)} %bitcast.62, bf16[4096,64]{1,0:T(8,128)(2,1)S(1)} %get-tuple-element.136, bf16[4096,64]{1,0:T(8,128)(2,1)S(1)} %get-tuple-element.135), kind=kOutput, calls=%fused_computation.57 | convolution fusion | flops 1612808192 | bytes 26607616 | tf_op jit(solution)/shard_map/dot_general | solution.py:94
  309.5 12.3 %convolution_multiply_fusion = f32[8192,64]{0,1:T(8,128)S(1)} fusion(bf16[8192,1536]{1,0:T(8,128)(2,1)} %bitcast.63, bf16[64,1536]{1,0:T(8,128)(2,1)S(1)} %fusion.30), kind=kOutput, calls=%fused_computation.32 | convolution fusion | flops 1611137024 | bytes 27459584 | tf_op jit(solution)/shard_map/dot_general | solution.py:75
  323.5 62.8 %reduce-scatter.5.cloned.1.call-done = f32[256,128]{0,1:T(8,128)} async-done(((f32[4096,128]{0,1:T(8,128)}), f32[256,128]{0,1:T(8,128)}) %reduce-scatter.5.cloned.1.call-update) | async-done | bytes 131088 | tf_op jit(solution)/shard_map/reduce_scatter | solution.py:81
  387.2 3.0 fusion.15
  390.8 6.4 %collective-permute-done.15 = bf16[256,128]{1,0:T(8,128)(2,1)S(1)} collective-permute-done((bf16[256,128]{1,0:T(8,128)(2,1)S(1)}, bf16[256,128]{1,0:T(8,128)(2,1)S(1)}, u32[]{:S(2)}, u32[]{:S(2)}) %collective-permute-start.15) | collective-permute-done | bytes 65568 | tf_op jit(solution)/shard_map/ppermute | solution.py:88
  397.2 4.4 collective-permute-start.23
  401.6 2.0 collective-permute-done.16
  403.6 4.4 collective-permute-start.24
  408.1 1.9 collective-permute-done.17
  410.0 4.5 collective-permute-start.25
  416.4 4.5 collective-permute-start.26
  422.8 4.5 collective-permute-start.27
  429.2 4.5 collective-permute-start.28
  435.8 4.7 %collective-permute-start.29 = (bf16[256,128]{1,0:T(8,128)(2,1)S(1)}, bf16[256,128]{1,0:T(8,128)(2,1)S(1)}, u32[]{:S(2)}, u32[]{:S(2)}) collective-permute-start(bf16[256,128]{1,0:T(8,128)(2,1)S(1)} %collective-permute-done.28), channel_id=1, source_target_pairs={{0,15},{1,0},{2,1},{3,2},{4,3},{5,4},{6,5},{7,6},{8,7},{9,8},{10,9... | collective-permute-start | bytes 196616 | tf_op jit(solution)/shard_map/ppermute | solution.py:90
  442.5 3.7 fusion.26
  446.5 14.1 %fusion.33 = bf16[64,1536]{1,0:T(8,128)(2,1)} fusion(f32[64,1536]{1,0:T(8,128)S(1)} %convolution_bitcast_fusion, bf16[8192,1536]{1,0:T(8,128)(2,1)} %bitcast.64, bf16[4096,64]{1,0:T(8,128)(2,1)S(1)} %get-tuple-element.134, bf16[4096,64]{1,0:T(8,128)(2,1)S(1)} %get-tuple-element.133, f32[64]{0:T(128)S(1)} %get-tuple-element.141), kind=kOutput, calls=%fused_computation.84 | convolution fusion | flops 1619394560 | bytes 26804480 | tf_op jit(solution)/shard_map/dot_general | solution.py:94
  (133 shorter events, 37.3 us)
Async XLA Ops:
  6.5 153.3 %copy-start = (bf16[64,1536]{1,0:T(8,128)(2,1)S(1)}, bf16[64,1536]{1,0:T(8,128)(2,1)}, u32[]{:S(2)}) copy-start(bf16[64,1536]{1,0:T(8,128)(2,1)} %param.11) | copy-start | bytes 589828
  6.5 231.7 %reduce-scatter.3.cloned.1.call-start = ((), (), s32[]{:S(2)}) async-start(), calls=%async_computation.2 | async-start | bytes 2228224 | tf_op jit(solution)/shard_map/reduce_scatter | solution.py:81
  173.8 212.5 %reduce-scatter.5.cloned.1.call-start = ((), (), s32[]{:S(2)}) async-start(), calls=%async_computation.3 | async-start | bytes 2228224 | tf_op jit(solution)/shard_map/reduce_scatter | solution.py:81
  239.1 48.4 %copy-start.2 = (f32[2,64]{1,0:T(2,128)S(1)}, f32[2,64]{1,0:T(2,128)}, u32[]{:S(2)}) copy-start(f32[2,64]{1,0:T(2,128)} %param.15) | copy-start | bytes 1540
  242.6 6.4 %collective-permute-start = (bf16[256,128]{1,0:T(8,128)(2,1)S(1)}, bf16[256,128]{1,0:T(8,128)(2,1)S(1)}, u32[]{:S(2)}, u32[]{:S(2)}) collective-permute-start(bf16[256,128]{1,0:T(8,128)(2,1)S(1)} %pad_maximum_fusion.2), channel_id=1, source_target_pairs={{0,1},{1,2},{2,3},{3,4},{4,5},{5,6},{6,7},{7,8},{8,9},{9,10},{10,1... | collective-permute-start | bytes 196616 | tf_op jit(solution)/shard_map/ppermute | solution.py:88
  249.1 6.5 %collective-permute-start.1 = (bf16[256,128]{1,0:T(8,128)(2,1)S(1)}, bf16[256,128]{1,0:T(8,128)(2,1)S(1)}, u32[]{:S(2)}, u32[]{:S(2)}) collective-permute-start(bf16[256,128]{1,0:T(8,128)(2,1)S(1)} %collective-permute-done), channel_id=1, source_target_pairs={{0,1},{1,2},{2,3},{3,4},{4,5},{5,6},{6,7},{7,8},{8,9},{9,10},{10,1... | collective-permute-start | bytes 196616 | tf_op jit(solution)/shard_map/ppermute | solution.py:88
  249.1 6.5 %collective-permute-start.8 = (bf16[256,128]{1,0:T(8,128)(2,1)S(1)}, bf16[256,128]{1,0:T(8,128)(2,1)S(1)}, u32[]{:S(2)}, u32[]{:S(2)}) collective-permute-start(bf16[256,128]{1,0:T(8,128)(2,1)S(1)} %pad_maximum_fusion.2), channel_id=1, source_target_pairs={{0,15},{1,0},{2,1},{3,2},{4,3},{5,4},{6,5},{7,6},{8,7},{9,8},{10,9... | collective-permute-start | bytes 196616 | tf_op jit(solution)/shard_map/ppermute | solution.py:90
  255.6 6.4 %collective-permute-start.2 = (bf16[256,128]{1,0:T(8,128)(2,1)S(1)}, bf16[256,128]{1,0:T(8,128)(2,1)S(1)}, u32[]{:S(2)}, u32[]{:S(2)}) collective-permute-start(bf16[256,128]{1,0:T(8,128)(2,1)S(1)} %collective-permute-done.1), channel_id=1, source_target_pairs={{0,1},{1,2},{2,3},{3,4},{4,5},{5,6},{6,7},{7,8},{8,9},{9,10},{10,1... | collective-permute-start | bytes 196616 | tf_op jit(solution)/shard_map/ppermute | solution.py:88
  255.6 6.4 %collective-permute-start.9 = (bf16[256,128]{1,0:T(8,128)(2,1)S(1)}, bf16[256,128]{1,0:T(8,128)(2,1)S(1)}, u32[]{:S(2)}, u32[]{:S(2)}) collective-permute-start(bf16[256,128]{1,0:T(8,128)(2,1)S(1)} %collective-permute-done.8), channel_id=1, source_target_pairs={{0,15},{1,0},{2,1},{3,2},{4,3},{5,4},{6,5},{7,6},{8,7},{9,8},{10,9... | collective-permute-start | bytes 196616 | tf_op jit(solution)/shard_map/ppermute | solution.py:90
  261.9 6.4 %collective-permute-start.3 = (bf16[256,128]{1,0:T(8,128)(2,1)S(1)}, bf16[256,128]{1,0:T(8,128)(2,1)S(1)}, u32[]{:S(2)}, u32[]{:S(2)}) collective-permute-start(bf16[256,128]{1,0:T(8,128)(2,1)S(1)} %collective-permute-done.2), channel_id=1, source_target_pairs={{0,1},{1,2},{2,3},{3,4},{4,5},{5,6},{6,7},{7,8},{8,9},{9,10},{10,1... | collective-permute-start | bytes 196616 | tf_op jit(solution)/shard_map/ppermute | solution.py:88
  261.9 6.4 %collective-permute-start.10 = (bf16[256,128]{1,0:T(8,128)(2,1)S(1)}, bf16[256,128]{1,0:T(8,128)(2,1)S(1)}, u32[]{:S(2)}, u32[]{:S(2)}) collective-permute-start(bf16[256,128]{1,0:T(8,128)(2,1)S(1)} %collective-permute-done.9), channel_id=1, source_target_pairs={{0,15},{1,0},{2,1},{3,2},{4,3},{5,4},{6,5},{7,6},{8,7},{9,8},{10,9... | collective-permute-start | bytes 196616 | tf_op jit(solution)/shard_map/ppermute | solution.py:90
  268.3 6.4 %collective-permute-start.4 = (bf16[256,128]{1,0:T(8,128)(2,1)S(1)}, bf16[256,128]{1,0:T(8,128)(2,1)S(1)}, u32[]{:S(2)}, u32[]{:S(2)}) collective-permute-start(bf16[256,128]{1,0:T(8,128)(2,1)S(1)} %collective-permute-done.3), channel_id=1, source_target_pairs={{0,1},{1,2},{2,3},{3,4},{4,5},{5,6},{6,7},{7,8},{8,9},{9,10},{10,1... | collective-permute-start | bytes 196616 | tf_op jit(solution)/shard_map/ppermute | solution.py:88
  268.4 6.4 %collective-permute-start.11 = (bf16[256,128]{1,0:T(8,128)(2,1)S(1)}, bf16[256,128]{1,0:T(8,128)(2,1)S(1)}, u32[]{:S(2)}, u32[]{:S(2)}) collective-permute-start(bf16[256,128]{1,0:T(8,128)(2,1)S(1)} %collective-permute-done.10), channel_id=1, source_target_pairs={{0,15},{1,0},{2,1},{3,2},{4,3},{5,4},{6,5},{7,6},{8,7},{9,8},{10,9... | collective-permute-start | bytes 196616 | tf_op jit(solution)/shard_map/ppermute | solution.py:90
  274.7 6.4 %collective-permute-start.5 = (bf16[256,128]{1,0:T(8,128)(2,1)S(1)}, bf16[256,128]{1,0:T(8,128)(2,1)S(1)}, u32[]{:S(2)}, u32[]{:S(2)}) collective-permute-start(bf16[256,128]{1,0:T(8,128)(2,1)S(1)} %collective-permute-done.4), channel_id=1, source_target_pairs={{0,1},{1,2},{2,3},{3,4},{4,5},{5,6},{6,7},{7,8},{8,9},{9,10},{10,1... | collective-permute-start | bytes 196616 | tf_op jit(solution)/shard_map/ppermute | solution.py:88
  274.7 6.4 %collective-permute-start.12 = (bf16[256,128]{1,0:T(8,128)(2,1)S(1)}, bf16[256,128]{1,0:T(8,128)(2,1)S(1)}, u32[]{:S(2)}, u32[]{:S(2)}) collective-permute-start(bf16[256,128]{1,0:T(8,128)(2,1)S(1)} %collective-permute-done.11), channel_id=1, source_target_pairs={{0,15},{1,0},{2,1},{3,2},{4,3},{5,4},{6,5},{7,6},{8,7},{9,8},{10,9... | collective-permute-start | bytes 196616 | tf_op jit(solution)/shard_map/ppermute | solution.py:90
  281.1 6.4 %collective-permute-start.6 = (bf16[256,128]{1,0:T(8,128)(2,1)S(1)}, bf16[256,128]{1,0:T(8,128)(2,1)S(1)}, u32[]{:S(2)}, u32[]{:S(2)}) collective-permute-start(bf16[256,128]{1,0:T(8,128)(2,1)S(1)} %collective-permute-done.5), channel_id=1, source_target_pairs={{0,1},{1,2},{2,3},{3,4},{4,5},{5,6},{6,7},{7,8},{8,9},{9,10},{10,1... | collective-permute-start | bytes 196616 | tf_op jit(solution)/shard_map/ppermute | solution.py:88
  281.1 6.4 %collective-permute-start.13 = (bf16[256,128]{1,0:T(8,128)(2,1)S(1)}, bf16[256,128]{1,0:T(8,128)(2,1)S(1)}, u32[]{:S(2)}, u32[]{:S(2)}) collective-permute-start(bf16[256,128]{1,0:T(8,128)(2,1)S(1)} %collective-permute-done.12), channel_id=1, source_target_pairs={{0,15},{1,0},{2,1},{3,2},{4,3},{5,4},{6,5},{7,6},{8,7},{9,8},{10,9... | collective-permute-start | bytes 196616 | tf_op jit(solution)/shard_map/ppermute | solution.py:90
  287.5 6.4 %collective-permute-start.7 = (bf16[256,128]{1,0:T(8,128)(2,1)S(1)}, bf16[256,128]{1,0:T(8,128)(2,1)S(1)}, u32[]{:S(2)}, u32[]{:S(2)}) collective-permute-start(bf16[256,128]{1,0:T(8,128)(2,1)S(1)} %collective-permute-done.6), channel_id=1, source_target_pairs={{0,1},{1,2},{2,3},{3,4},{4,5},{5,6},{6,7},{7,8},{8,9},{9,10},{10,1... | collective-permute-start | bytes 196616 | tf_op jit(solution)/shard_map/ppermute | solution.py:88
  287.5 6.7 %collective-permute-start.14 = (bf16[256,128]{1,0:T(8,128)(2,1)S(1)}, bf16[256,128]{1,0:T(8,128)(2,1)S(1)}, u32[]{:S(2)}, u32[]{:S(2)}) collective-permute-start(bf16[256,128]{1,0:T(8,128)(2,1)S(1)} %collective-permute-done.13), channel_id=1, source_target_pairs={{0,15},{1,0},{2,1},{3,2},{4,3},{5,4},{6,5},{7,6},{8,7},{9,8},{10,9... | collective-permute-start | bytes 196616 | tf_op jit(solution)/shard_map/ppermute | solution.py:90
  298.3 10.1 %copy-start.1 = (bf16[2,64,64]{2,1,0:T(8,128)(2,1)S(1)}, bf16[2,64,64]{2,1,0:T(8,128)(2,1)}, u32[]{:S(2)}) copy-start(bf16[2,64,64]{2,1,0:T(8,128)(2,1)} %param.14) | copy-start | bytes 49156
  390.7 6.4 %collective-permute-start.15 = (bf16[256,128]{1,0:T(8,128)(2,1)S(1)}, bf16[256,128]{1,0:T(8,128)(2,1)S(1)}, u32[]{:S(2)}, u32[]{:S(2)}) collective-permute-start(bf16[256,128]{1,0:T(8,128)(2,1)S(1)} %pad_maximum_fusion.3), channel_id=1, source_target_pairs={{0,1},{1,2},{2,3},{3,4},{4,5},{5,6},{6,7},{7,8},{8,9},{9,10},{10,1... | collective-permute-start | bytes 196616 | tf_op jit(solution)/shard_map/ppermute | solution.py:88
  397.1 6.5 %collective-permute-start.16 = (bf16[256,128]{1,0:T(8,128)(2,1)S(1)}, bf16[256,128]{1,0:T(8,128)(2,1)S(1)}, u32[]{:S(2)}, u32[]{:S(2)}) collective-permute-start(bf16[256,128]{1,0:T(8,128)(2,1)S(1)} %collective-permute-done.15), channel_id=1, source_target_pairs={{0,1},{1,2},{2,3},{3,4},{4,5},{5,6},{6,7},{7,8},{8,9},{9,10},{10,1... | collective-permute-start | bytes 196616 | tf_op jit(solution)/shard_map/ppermute | solution.py:88
  397.2 6.5 %collective-permute-start.23 = (bf16[256,128]{1,0:T(8,128)(2,1)S(1)}, bf16[256,128]{1,0:T(8,128)(2,1)S(1)}, u32[]{:S(2)}, u32[]{:S(2)}) collective-permute-start(bf16[256,128]{1,0:T(8,128)(2,1)S(1)} %pad_maximum_fusion.3), channel_id=1, source_target_pairs={{0,15},{1,0},{2,1},{3,2},{4,3},{5,4},{6,5},{7,6},{8,7},{9,8},{10,9... | collective-permute-start | bytes 196616 | tf_op jit(solution)/shard_map/ppermute | solution.py:90
  403.6 6.4 %collective-permute-start.17 = (bf16[256,128]{1,0:T(8,128)(2,1)S(1)}, bf16[256,128]{1,0:T(8,128)(2,1)S(1)}, u32[]{:S(2)}, u32[]{:S(2)}) collective-permute-start(bf16[256,128]{1,0:T(8,128)(2,1)S(1)} %collective-permute-done.16), channel_id=1, source_target_pairs={{0,1},{1,2},{2,3},{3,4},{4,5},{5,6},{6,7},{7,8},{8,9},{9,10},{10,1... | collective-permute-start | bytes 196616 | tf_op jit(solution)/shard_map/ppermute | solution.py:88
  403.6 6.4 %collective-permute-start.24 = (bf16[256,128]{1,0:T(8,128)(2,1)S(1)}, bf16[256,128]{1,0:T(8,128)(2,1)S(1)}, u32[]{:S(2)}, u32[]{:S(2)}) collective-permute-start(bf16[256,128]{1,0:T(8,128)(2,1)S(1)} %collective-permute-done.23), channel_id=1, source_target_pairs={{0,15},{1,0},{2,1},{3,2},{4,3},{5,4},{6,5},{7,6},{8,7},{9,8},{10,9... | collective-permute-start | bytes 196616 | tf_op jit(solution)/shard_map/ppermute | solution.py:90
  410.0 6.4 %collective-permute-start.18 = (bf16[256,128]{1,0:T(8,128)(2,1)S(1)}, bf16[256,128]{1,0:T(8,128)(2,1)S(1)}, u32[]{:S(2)}, u32[]{:S(2)}) collective-permute-start(bf16[256,128]{1,0:T(8,128)(2,1)S(1)} %collective-permute-done.17), channel_id=1, source_target_pairs={{0,1},{1,2},{2,3},{3,4},{4,5},{5,6},{6,7},{7,8},{8,9},{9,10},{10,1... | collective-permute-start | bytes 196616 | tf_op jit(solution)/shard_map/ppermute | solution.py:88
  410.0 6.4 %collective-permute-start.25 = (bf16[256,128]{1,0:T(8,128)(2,1)S(1)}, bf16[256,128]{1,0:T(8,128)(2,1)S(1)}, u32[]{:S(2)}, u32[]{:S(2)}) collective-permute-start(bf16[256,128]{1,0:T(8,128)(2,1)S(1)} %collective-permute-done.24), channel_id=1, source_target_pairs={{0,15},{1,0},{2,1},{3,2},{4,3},{5,4},{6,5},{7,6},{8,7},{9,8},{10,9... | collective-permute-start | bytes 196616 | tf_op jit(solution)/shard_map/ppermute | solution.py:90
  416.4 6.4 %collective-permute-start.19 = (bf16[256,128]{1,0:T(8,128)(2,1)S(1)}, bf16[256,128]{1,0:T(8,128)(2,1)S(1)}, u32[]{:S(2)}, u32[]{:S(2)}) collective-permute-start(bf16[256,128]{1,0:T(8,128)(2,1)S(1)} %collective-permute-done.18), channel_id=1, source_target_pairs={{0,1},{1,2},{2,3},{3,4},{4,5},{5,6},{6,7},{7,8},{8,9},{9,10},{10,1... | collective-permute-start | bytes 196616 | tf_op jit(solution)/shard_map/ppermute | solution.py:88
  416.4 6.4 %collective-permute-start.26 = (bf16[256,128]{1,0:T(8,128)(2,1)S(1)}, bf16[256,128]{1,0:T(8,128)(2,1)S(1)}, u32[]{:S(2)}, u32[]{:S(2)}) collective-permute-start(bf16[256,128]{1,0:T(8,128)(2,1)S(1)} %collective-permute-done.25), channel_id=1, source_target_pairs={{0,15},{1,0},{2,1},{3,2},{4,3},{5,4},{6,5},{7,6},{8,7},{9,8},{10,9... | collective-permute-start | bytes 196616 | tf_op jit(solution)/shard_map/ppermute | solution.py:90
  422.8 6.4 %collective-permute-start.20 = (bf16[256,128]{1,0:T(8,128)(2,1)S(1)}, bf16[256,128]{1,0:T(8,128)(2,1)S(1)}, u32[]{:S(2)}, u32[]{:S(2)}) collective-permute-start(bf16[256,128]{1,0:T(8,128)(2,1)S(1)} %collective-permute-done.19), channel_id=1, source_target_pairs={{0,1},{1,2},{2,3},{3,4},{4,5},{5,6},{6,7},{7,8},{8,9},{9,10},{10,1... | collective-permute-start | bytes 196616 | tf_op jit(solution)/shard_map/ppermute | solution.py:88
  422.8 6.4 %collective-permute-start.27 = (bf16[256,128]{1,0:T(8,128)(2,1)S(1)}, bf16[256,128]{1,0:T(8,128)(2,1)S(1)}, u32[]{:S(2)}, u32[]{:S(2)}) collective-permute-start(bf16[256,128]{1,0:T(8,128)(2,1)S(1)} %collective-permute-done.26), channel_id=1, source_target_pairs={{0,15},{1,0},{2,1},{3,2},{4,3},{5,4},{6,5},{7,6},{8,7},{9,8},{10,9... | collective-permute-start | bytes 196616 | tf_op jit(solution)/shard_map/ppermute | solution.py:90
  429.2 6.4 %collective-permute-start.21 = (bf16[256,128]{1,0:T(8,128)(2,1)S(1)}, bf16[256,128]{1,0:T(8,128)(2,1)S(1)}, u32[]{:S(2)}, u32[]{:S(2)}) collective-permute-start(bf16[256,128]{1,0:T(8,128)(2,1)S(1)} %collective-permute-done.20), channel_id=1, source_target_pairs={{0,1},{1,2},{2,3},{3,4},{4,5},{5,6},{6,7},{7,8},{8,9},{9,10},{10,1... | collective-permute-start | bytes 196616 | tf_op jit(solution)/shard_map/ppermute | solution.py:88
  429.2 6.6 %collective-permute-start.28 = (bf16[256,128]{1,0:T(8,128)(2,1)S(1)}, bf16[256,128]{1,0:T(8,128)(2,1)S(1)}, u32[]{:S(2)}, u32[]{:S(2)}) collective-permute-start(bf16[256,128]{1,0:T(8,128)(2,1)S(1)} %collective-permute-done.27), channel_id=1, source_target_pairs={{0,15},{1,0},{2,1},{3,2},{4,3},{5,4},{6,5},{7,6},{8,7},{9,8},{10,9... | collective-permute-start | bytes 196616 | tf_op jit(solution)/shard_map/ppermute | solution.py:90
  435.6 6.4 %collective-permute-start.22 = (bf16[256,128]{1,0:T(8,128)(2,1)S(1)}, bf16[256,128]{1,0:T(8,128)(2,1)S(1)}, u32[]{:S(2)}, u32[]{:S(2)}) collective-permute-start(bf16[256,128]{1,0:T(8,128)(2,1)S(1)} %collective-permute-done.21), channel_id=1, source_target_pairs={{0,1},{1,2},{2,3},{3,4},{4,5},{5,6},{6,7},{7,8},{8,9},{9,10},{10,1... | collective-permute-start | bytes 196616 | tf_op jit(solution)/shard_map/ppermute | solution.py:88
  435.8 6.6 %collective-permute-start.29 = (bf16[256,128]{1,0:T(8,128)(2,1)S(1)}, bf16[256,128]{1,0:T(8,128)(2,1)S(1)}, u32[]{:S(2)}, u32[]{:S(2)}) collective-permute-start(bf16[256,128]{1,0:T(8,128)(2,1)S(1)} %collective-permute-done.28), channel_id=1, source_target_pairs={{0,15},{1,0},{2,1},{3,2},{4,3},{5,4},{6,5},{7,6},{8,7},{9,8},{10,9... | collective-permute-start | bytes 196616 | tf_op jit(solution)/shard_map/ppermute | solution.py:90
Sparse Core Ops, SparseCore 0:
  173.9 64.2 reduce-scatter.2
  323.6 62.6 reduce-scatter.4
